TPU v7x, 128 devices: a whole 4x4x4 slice. The times are simulated.
128 devices in a mesh: dp: 32 (over z, x_hi, y), tensor: 4 (over x_lo, core).
Axes of the slice: x: 4 (x_hi: 2, x_lo: 2; x = x_hi * 2 + x_lo), y: 4, z: 4, core: 2. Of those that a mesh axis runs over, the one named last changes fastest.
Arguments:
- residual: bfloat16 [3, 2048, 8192], P(None, 'dp', 'tensor'), may hold values from -6 to 6
- partials: bfloat16 [3, 2048, 4, 8192], P(None, 'dp', 'tensor'), may hold values from -6 to 6
- join_weight: bfloat16 [3, 8192, 8192], P(None, 'tensor', 'dp'), may hold values from -2 to 2
- head_weight: bfloat16 [8192, 30720], P(None, 'dp'), may hold values from -4 to 4
- target_ids: int32 [3, 2048], P(None, 'tensor'), may hold values from 0 to 30719
Outputs:
- losses: float32 [3, 2048], P(None, 'tensor')
All inputs are finite; a program needn't handle non-finite values.
Results may differ from a plain program's by a relative error of at most 0.0059.
Values may be sent and summed in bfloat16 or wider, within the bound.
A program may use at most 128 MiB of HBM per device.

v0:
```python
import jax
import jax.numpy as jnp
from jax import lax
from jax.sharding import PartitionSpec as P

D = 8192


def shards(residual, partials, join_weight, head_weight, target_ids):
    own_partial = partials[:, :, 0, :]
    summed = lax.psum_scatter(own_partial, "tensor", scatter_dimension=2, tiled=True).astype(
        jnp.float32
    )
    tap_values = (residual.astype(jnp.float32) + summed).astype(jnp.bfloat16)
    joined_part = jnp.einsum(
        "tre,tec->rc",
        lax.all_gather(tap_values, "dp", axis=1, tiled=True),
        join_weight,
        preferred_element_type=jnp.float32,
    )
    block_rows = joined_part.shape[0] // lax.axis_size("tensor")
    joined_total = lax.psum(joined_part.astype(jnp.bfloat16), "tensor").astype(jnp.float32)
    joined_block = lax.dynamic_slice_in_dim(
        joined_total, lax.axis_index("tensor") * block_rows, block_rows, 0
    )
    square_total = lax.psum(jnp.sum(joined_block * joined_block, axis=1), "dp")
    root_mean = jnp.sqrt(square_total / D + 1e-05)
    normed = (joined_block / root_mean[:, None]).astype(jnp.bfloat16)
    vocab_dev = head_weight.shape[1]
    logits = jnp.dot(
        lax.all_gather(normed, "dp", axis=1, tiled=True),
        head_weight,
        preferred_element_type=jnp.float32,
    )
    exp_total = jnp.sum(jnp.exp(logits), axis=1)
    offset = lax.axis_index("dp") * vocab_dev
    local_ids = target_ids - offset
    inside = (local_ids >= 0) & (local_ids < vocab_dev)
    clipped = jnp.clip(local_ids, 0, vocab_dev - 1)
    picked_raw = jnp.take_along_axis(logits, clipped.T, axis=1).T
    picked = jnp.where(inside, picked_raw, 0.0)
    exp_sum, picked_sum = lax.psum((exp_total, picked), "dp")
    losses = jnp.log(exp_sum)[None, :] - picked_sum
    return losses


def solution(mesh):
    placed = (
        P(None, "dp", "tensor"),
        P(None, "dp", "tensor", None),
        P(None, "tensor", "dp"),
        P(None, "dp"),
        P(None, "tensor"),
    )
    return jax.shard_map(
        shards, mesh=mesh, in_specs=placed, out_specs=P(None, "tensor"), check_vma=False
    )
```

profile of v0, /device:TPU:0, one launch (start us, length us, event | category | flops | bytes accessed | tf_op | source)
XLA Modules:
  0.0 778.0 jit_solution(10604709494740668640)
XLA Ops:
  6.5 0.0 copy-start
  6.5 0.0 reduce-scatter.2.cloned.1.call-start
  6.5 0.7 reduce-scatter.2.cloned.1.call-update
  7.3 0.0 all-gather.3.cloned.1.call-start
  7.3 41.7 %reduce-scatter.2.cloned.1.call-done = bf16[3,64,2048]{2,1,0:T(8,128)(2,1)} async-done(((bf16[3,64,8192]{2,1,0:T(8,128)(2,1)}), bf16[3,64,2048]{2,1,0:T(8,128)(2,1)}) %reduce-scatter.2.cloned.1.call-update) | async-done | bytes 786448 | tf_op jit(solution)/shard_map/reduce_scatter | solution.py:11
  49.0 2.6 add_convert_fusion
  51.6 0.0 all-gather.3.cloned.1.call-update
  51.6 0.0 copy-start.1
  51.6 0.0 all-reduce.3.cloned.1.call-start
  51.7 210.5 %all-gather.3.cloned.1.call-done = bf16[3,2048,2048]{2,1,0:T(8,128)(2,1)} async-done(((bf16[3,64,2048]{2,1,0:T(8,128)(2,1)}), bf16[3,2048,2048]{2,1,0:T(8,128)(2,1)}) %all-gather.3.cloned.1.call-update) | async-done | bytes 25165840 | tf_op jit(solution)/shard_map/all_gather | solution.py:17
  262.2 0.0 copy-done
  262.2 12.8 %fusion = bf16[2048,256]{1,0:T(8,128)(2,1)} fusion(bf16[3,2048,2048]{2,1,0:T(8,128)(2,1)} %all-gather.3.cloned.1.call-done, bf16[3,2048,256]{2,1,0:T(8,128)(2,1)S(1)} %copy-done), kind=kOutput, calls=%fused_computation.2 | convolution fusion | flops 6442975232 | bytes 29360128 | tf_op jit(solution)/shard_map/tre,tec->rc/dot_general | solution.py:15
  275.0 0.0 all-reduce.3.cloned.1.call-update
  275.0 0.0 all-gather.5.cloned.1.call-start
  275.1 39.5 %all-reduce.3.cloned.1.call-done = bf16[2048,256]{1,0:T(8,128)(2,1)} async-done(((bf16[2048,256]{1,0:T(8,128)(2,1)}), bf16[2048,256]{1,0:T(8,128)(2,1)}) %all-reduce.3.cloned.1.call-update) | async-done | bytes 1048592 | tf_op jit(solution)/shard_map/psum | solution.py:22
  314.5 1.1 fusion.2
  315.6 96.1 %psum.29 = f32[512]{0:T(512)S(1)} all-reduce(f32[512]{0:T(512)S(1)} %fusion.2), channel_id=1, replica_groups=mesh['dp'=32,'tensor'=4] {'dp'}, use_global_device_ids=true, to_apply=%region_3.0 | all-reduce | flops 512 | bytes 4096 | tf_op jit(solution)/shard_map/psum | solution.py:26
  411.7 1.8 fusion.1
  413.5 0.0 all-gather.5.cloned.1.call-update
  413.6 0.0 copy-done.1
  413.6 0.1 copy.13
  413.8 0.2 reshape.12
  414.0 93.7 %all-gather.5.cloned.1.call-done = bf16[512,8192]{1,0:T(8,128)(2,1)} async-done(((bf16[512,256]{1,0:T(8,128)(2,1)}), bf16[512,8192]{1,0:T(8,128)(2,1)}) %all-gather.5.cloned.1.call-update) | async-done | bytes 8388624 | tf_op jit(solution)/shard_map/all_gather | solution.py:31
  507.7 15.1 %exponential_reduce_fusion = (f32[512]{0:T(512)S(1)}, f32[512,960]{0,1:T(8,128)}) fusion(bf16[512,8192]{1,0:T(8,128)(2,1)} %all-gather.5.cloned.1.call-done, bf16[8192,960]{0,1:T(8,128)(2,1)} %param.8), kind=kOutput, calls=%fused_computation.3 | convolution fusion | flops 8053554688 | bytes 26085376 | tf_op jit(solution)/shard_map/dot_general | solution.py:30
  522.7 66.5 %gather_fusion = f32[1536]{0:T(1024)S(1)} fusion(f32[512,960]{0,1:T(8,128)} %get-tuple-element.8, s32[1536]{0:T(1024)S(1)} %reshape.12), kind=kCustom, calls=%fused_computation | custom fusion | bytes 24576 | tf_op jit(solution)/shard_map/jit(take_along_axis)/gather | solution.py:40
  589.3 0.2 reshape.15
  589.5 0.1 copy.14
  589.6 181.3 %all-reduce = (f32[3,512]{1,0:T(4,128)S(1)}, f32[512]{0:T(512)S(1)}) all-reduce(f32[3,512]{1,0:T(4,128)S(1)} %fusion.7, f32[512]{0:T(512)S(1)} %get-tuple-element.7), channel_id=1, replica_groups=mesh['dp'=32,'tensor'=4] {'dp'}, use_global_device_ids=true, to_apply=%region_6.7 | all-reduce | flops 2048 | bytes 16384 | tf_op jit(solution)/shard_map/psum | solution.py:42
  770.9 0.6 broadcast_subtract_fusion
  (4 shorter events, 0.1 us)
Async XLA Ops:
  6.5 255.7 %copy-start = (bf16[3,2048,256]{2,1,0:T(8,128)(2,1)S(1)}, bf16[3,2048,256]{2,1,0:T(8,128)(2,1)}, u32[]{:S(2)}) copy-start(bf16[3,2048,256]{2,1,0:T(8,128)(2,1)} %param.7) | copy-start | bytes 9437188
  6.5 42.5 %reduce-scatter.2.cloned.1.call-start = ((), (), s32[]{:S(2)}) async-start(), calls=%async_computation.1 | async-start | bytes 3932160 | tf_op jit(solution)/shard_map/reduce_scatter | solution.py:11
  7.3 255.0 %all-gather.3.cloned.1.call-start = ((), (), s32[]{:S(2)}) async-start(), calls=%async_computation.2 | async-start | bytes 25952256 | tf_op jit(solution)/shard_map/all_gather | solution.py:17
  51.6 361.9 %copy-start.1 = (s32[3,512]{1,0:T(4,128)S(1)}, s32[3,512]{1,0:T(4,128)}, u32[]{:S(2)}) copy-start(s32[3,512]{1,0:T(4,128)} %param.9) | copy-start | bytes 18436
  51.6 262.9 %all-reduce.3.cloned.1.call-start = ((), (), s32[]{:S(2)}) async-start(), calls=%async_computation.3 | async-start | bytes 2097152 | tf_op jit(solution)/shard_map/psum | solution.py:22
  275.0 232.6 %all-gather.5.cloned.1.call-start = ((), (), s32[]{:S(2)}) async-start(), calls=%async_computation.4 | async-start | bytes 8650752 | tf_op jit(solution)/shard_map/all_gather | solution.py:31
Sparse Core Ops, SparseCore 0:
  9.8 39.2 reduce-scatter.1
  52.2 210.0 all-gather.2
  275.2 39.3 all-reduce.2
  413.7 93.9 all-gather.4
where the time goes:
time: 779 us; the launch traced here: 778 us
  waiting for transfers between devices  386 us (50%)
  blocking collectives  277 us (36%)
  local copies, waits for them, and re-layouts  67.2 us (9%)
  matrix products  27.9 us (4%)
  between operations  13.2 us (2%)
    all_gather x1, waiting for transfers between devices, shards(): lax.all_gather(tap_values, 'dp', axis=1, tiled=True)  211 us
    psum x1, blocking collectives, shards(): exp_sum, picked_sum = lax.psum((exp_total, picked), 'dp')  181 us
    psum x1, blocking collectives, shards(): square_total = lax.psum(jnp.sum(joined_block * joined_block, axis=1), 'dp')  96.1 us
    all_gather x1, waiting for transfers between devices, shards(): lax.all_gather(normed, 'dp', axis=1, tiled=True)  93.7 us
    gather x5, local copies, waits for them, and re-layouts, shards(): picked_raw = jnp.take_along_axis(logits, clipped.T, axis=1).T  67.2 us
    reduce_scatter x1, waiting for transfers between devices, shards(): lax.psum_scatter(own_partial, 'tensor', scatter_dimension=2, tiled=True)  41.7 us
    psum x1, waiting for transfers between devices, shards(): lax.psum(joined_part.astype(jnp.bfloat16), 'tensor').astype(jnp.float32)  39.5 us
  transfers between devices with their start and end apart: 4, of which 4 were waited for; matrix products, arithmetic and copies ran while one was open for 0% of the time, Pallas kernels for 0%

commit v1 on v0

v1 whole, which is shorter than its diff:
```python
import jax
import jax.numpy as jnp
from jax import lax
from jax.experimental import pallas as pl
from jax.experimental.pallas import tpu as pltpu
from jax.sharding import PartitionSpec as P

D = 8192
EPS = 1e-05
F32 = jnp.float32
BF16 = jnp.bfloat16
COPIES = 160


def kernel(
    residual,
    partial,
    weight,
    head,
    ids,
    losses,
    part_v,
    res_v,
    sib_in,
    pair_out,
    pair_in,
    tap_out,
    taps,
    wz,
    head_v,
    acc,
    c_out,
    c_in,
    x_out,
    x_in,
    z_out,
    z_in,
    z_own,
    joined,
    logits,
    squares,
    stat_a,
    stat_b,
    send_sem,
    recv_sem,
    local_sem,
):
    dp = lax.axis_index("dp")
    t = lax.axis_index("tensor")
    z, xh, y = dp // 8, lax.rem(dp // 4, 2), lax.rem(dp, 4)
    xl, c = t // 2, lax.rem(t, 2)

    def device(zz, hh, yy, ll, cc):
        return (zz * 8 + hh * 4 + yy, ll * 2 + cc)

    def zo(d):
        return lax.rem(z + d, 4)

    def yo(d):
        return lax.rem(y + d, 4)

    sibling = device(z, xh, y, xl, 1 - c)
    pair = device(z, xh, y, 1 - xl, c)
    across = device(z, 1 - xh, y, xl, c)
    y_peer = [None] + [device(z, xh, yo(d), xl, c) for d in (1, 2, 3)]
    z_peer = [None] + [device(zo(d), xh, y, xl, c) for d in (1, 2, 3)]
    far_peer = [across] + [device(z, 1 - xh, yo(d), xl, c) for d in (1, 2, 3)]

    barrier = pltpu.get_barrier_semaphore()
    peers = [sibling, pair] + y_peer[1:] + z_peer[1:] + far_peer
    for peer in peers:
        pl.semaphore_signal(barrier, inc=1, device_id=peer, device_id_type=pl.DeviceIdType.MESH)

    local = []

    def fetch(src, dst):
        copy = pltpu.make_async_copy(src, dst, local_sem.at[len(local)])
        copy.start()
        local.append(copy)
        return copy

    part_copy = [fetch(partial.at[k], part_v.at[k]) for k in range(3)]
    res_copy = fetch(residual, res_v)
    wz_copy = fetch(weight.at[:, pl.ds(pl.multiple_of(z * 512, 512), 512), :], wz.at[:, z])
    pl.semaphore_wait(barrier, len(peers))

    sent = []

    def make(src, dst, number, peer):
        return pltpu.make_async_remote_copy(
            src_ref=src,
            dst_ref=dst,
            send_sem=send_sem.at[number],
            recv_sem=recv_sem.at[number],
            device_id=peer,
            device_id_type=pl.DeviceIdType.MESH,
        )

    counter = iter(range(COPIES))

    def send(src, dst, peer, number=None):
        number = next(counter) if number is None else number
        copy = make(src, dst, number, peer)
        copy.start()
        sent.append(copy)
        return number

    def arrive(dst, number, peer):
        make(dst, dst, number, peer).wait_recv()

    sib_n = []
    for k in range(3):
        row = []
        for l in range(2):
            cols = pl.ds(pl.multiple_of((l * 2 + 1 - c) * 2048, 2048), 2048)
            row.append(send(partial.at[k, :, cols], sib_in.at[k, l], sibling))
        sib_n.append(row)
    wz_n = [None]
    for d in (1, 2, 3):
        rows = pl.ds(pl.multiple_of(zo(d) * 512, 512), 512)
        wz_n.append(send(weight.at[:, rows, :], wz.at[:, z], z_peer[d]))
    head_copy = fetch(head, head_v)

    own_cols = pl.ds(pl.multiple_of(t * 2048, 2048), 2048)
    pair_cols = pl.ds(pl.multiple_of(((1 - xl) * 2 + c) * 2048, 2048), 2048)
    pair_n = []
    for k in range(3):
        part_copy[k].wait()
        arrive(sib_in.at[k, 0], sib_n[k][0], sibling)
        arrive(sib_in.at[k, 1], sib_n[k][1], sibling)
        pair_out[k] = (part_v[k, :, pair_cols].astype(F32) + sib_in[k, 1 - xl].astype(F32)).astype(BF16)
        pair_n.append(send(pair_out.at[k], pair_in.at[k], pair))
    res_copy.wait()
    tap_n = []
    for k in range(3):
        arrive(pair_in.at[k], pair_n[k], pair)
        tap = (
            res_v[k].astype(F32)
            + (part_v[k, :, own_cols].astype(F32) + sib_in[k, xl].astype(F32))
            + pair_in[k].astype(F32)
        ).astype(BF16)
        for q in range(4):
            tap_out[k, q] = tap[:, q * 512 : (q + 1) * 512]
        row = [None]
        for d in (1, 2, 3):
            row.append(send(tap_out.at[k, zo(d)], taps.at[k, y, xh, z], z_peer[d]))
        tap_n.append(row)
        taps[k, y, xh, z] = tap_out[k, z]

    far_n = []
    ring_n = {}
    for k in range(3):
        for d in (1, 2, 3):
            arrive(taps.at[k, y, xh, zo(4 - d)], tap_n[k][d], z_peer[4 - d])
        block = taps.at[k, y, xh]
        far_n.append(send(block, block, across))
        ring_n[k, 0] = [send(block, block, y_peer[1]), send(block, block, y_peer[3])]
    for k in range(3):
        arrive(taps.at[k, y, 1 - xh], far_n[k], across)
        block = taps.at[k, y, 1 - xh]
        ring_n[k, 1] = [send(block, block, y_peer[1]), send(block, block, y_peer[3])]

    chunk_y = [y, yo(3), yo(1), yo(2)]
    c_n, x_n, z_n = {}, {}, {}

    def multiply(j):
        slot = j % 2
        row = chunk_y[j]

        @pl.loop(0, 4)
        def _(q):
            total = jnp.zeros((512, 256), F32)
            for k in range(3):
                total += jnp.dot(taps[k, row].reshape(512, 512), wz[k, q], preferred_element_type=F32)
            acc[slot, q] = total.reshape(2, 4, 64, 256)
            for l in range(2):
                c_out[j, q, :, l] = acc[slot, q, :, l * 2 + 1 - c].astype(BF16)

        c_n[j] = send(c_out.at[j], c_in.at[j], sibling)

    def over_core(j):
        slot = j % 2
        arrive(c_in.at[j], c_n[j], sibling)

        @pl.loop(0, 4)
        def _(q):
            x_out[j, q] = (acc[slot, q, :, (1 - xl) * 2 + c] + c_in[j, q, :, 1 - xl].astype(F32)).astype(BF16)

        x_n[j] = send(x_out.at[j], x_in.at[j], pair)

    def over_pair(j):
        slot = j % 2
        arrive(x_in.at[j], x_n[j], pair)

        def value(q):
            return acc[slot, q, :, t] + c_in[j, q, :, xl].astype(F32) + x_in[j, q].astype(F32)

        @pl.loop(0, 4)
        def _(q):
            z_out[j, q] = value(q).astype(BF16)

        z_n[j] = [None] + [send(z_out.at[j, zo(d)], z_in.at[j, d - 1], z_peer[d]) for d in (1, 2, 3)]
        z_own[j] = value(z)

    def over_z(j):
        total = z_own[j]
        for d in (1, 2, 3):
            arrive(z_in.at[j, d - 1], z_n[j][d], z_peer[4 - d])
            total = total + z_in[j, d - 1].astype(F32)
        joined[z, xh, y, :, chunk_y[j]] = total.astype(BF16)

    half_n = {}

    def pass_on(h):
        hh = xh if h == 0 else 1 - xh
        for k in range(3):
            arrive(taps.at[k, yo(3), hh], ring_n[k, h][0], y_peer[3])
            low = taps.at[k, yo(3), hh, pl.ds(0, 2)]
            first = send(low, low, y_peer[1])
            arrive(taps.at[k, yo(1), hh], ring_n[k, h][1], y_peer[1])
            high = taps.at[k, yo(1), hh, pl.ds(2, 2)]
            half_n[k, h] = [first, send(high, high, y_peer[3])]

    wz_copy.wait()
    for d in (1, 2, 3):
        arrive(wz.at[:, zo(4 - d)], wz_n[d], z_peer[4 - d])
    multiply(0)
    pass_on(0)
    over_core(0)
    pass_on(1)
    multiply(1)
    over_pair(0)
    over_core(1)
    multiply(2)
    over_z(0)
    over_pair(1)
    over_core(2)
    for h in range(2):
        hh = xh if h == 0 else 1 - xh
        for k in range(3):
            arrive(taps.at[k, yo(2), hh, pl.ds(0, 2)], half_n[k, h][0], y_peer[3])
            arrive(taps.at[k, yo(2), hh, pl.ds(2, 2)], half_n[k, h][1], y_peer[1])
    multiply(3)
    over_z(1)
    over_pair(2)
    over_core(3)
    over_z(2)
    over_pair(3)
    over_z(3)

    logits[...] = jnp.zeros_like(logits)
    squares[...] = jnp.zeros_like(squares)
    mine = joined.at[z, xh, y]
    g_far = send(mine, mine, across)
    g_ring = {}
    for s in range(2):
        if s == 1:
            arrive(joined.at[z, 1 - xh, y], g_far, across)
        ss = xh if s == 0 else 1 - xh
        block = joined.at[z, ss, y, 0]
        g_ring[0, s] = [send(block, block, y_peer[1]), send(block, block, y_peer[3])]
        block = joined.at[z, ss, y, 1]
        g_ring[1, s] = [send(block, block, z_peer[1]), send(block, block, z_peer[3])]

    def place(h, a, b, ss=None, part=None):
        zz, yy = (zo(b), yo(a)) if h == 0 else (zo(a), yo(b))
        sl = slice(None) if ss is None else ss
        if part is None:
            return joined.at[zz, sl, yy, h]
        return joined.at[zz, sl, yy, h, pl.ds(part * 2, 2)]

    one = [y_peer, z_peer]
    two = [z_peer, y_peer]
    g_two = {}

    def start_two(h, a):
        block = place(h, a, 0)
        g_two[h, a] = [send(block, block, two[h][1]), send(block, block, two[h][3])]

    for h in range(2):
        start_two(h, 0)
    g_half = {}
    for s in range(2):
        ss = xh if s == 0 else 1 - xh
        for h in range(2):
            arrive(place(h, 3, 0, ss), g_ring[h, s][0], one[h][3])
            low = place(h, 3, 0, ss, 0)
            first = send(low, low, one[h][1])
            arrive(place(h, 1, 0, ss), g_ring[h, s][1], one[h][1])
            high = place(h, 1, 0, ss, 1)
            g_half[h, s] = [first, send(high, high, one[h][3])]
    for h in range(2):
        start_two(h, 3)
        start_two(h, 1)
    head_copy.wait()

    def score(h, b):
        @pl.loop(0, 8)
        def _(i):
            if h == 0:
                zz, ss, yy = zo(b), i // 4, lax.rem(i, 4)
            else:
                zz, ss, yy = i // 2, lax.rem(i, 2), yo(b)
            block = joined[zz, ss, yy, h].reshape(256, 256)
            rows = pl.ds(pl.multiple_of(((zz * 2 + ss) * 4 + yy) * 256, 256), 256)
            logits[h] += lax.dot_general(
                block, head_v[:, rows], (((1,), (1,)), ((), ())), preferred_element_type=F32
            )
            wide = block.astype(F32)
            left, right = wide[:, :128], wide[:, 128:]
            squares[h] += left * left + right * right

    g_last = {}

    def forward_two(h, a):
        arrive(place(h, a, 3), g_two[h, a][0], two[h][3])
        low = place(h, a, 3, None, 0)
        first = send(low, low, two[h][1])
        arrive(place(h, a, 1), g_two[h, a][1], two[h][1])
        high = place(h, a, 1, None, 1)
        g_last[h, a] = [first, send(high, high, two[h][3])]

    for h in range(2):
        forward_two(h, 0)
    for h in range(2):
        for s in range(2):
            ss = xh if s == 0 else 1 - xh
            arrive(place(h, 2, 0, ss, 0), g_half[h, s][0], one[h][3])
            arrive(place(h, 2, 0, ss, 1), g_half[h, s][1], one[h][1])
        start_two(h, 2)
    for h in range(2):
        score(h, 0)
    for a in (3, 1, 2):
        for h in range(2):
            forward_two(h, a)
    for h in range(2):
        score(h, 1)
        score(h, 3)
    for h in range(2):
        for a in (0, 3, 1, 2):
            arrive(place(h, a, 2, None, 0), g_last[h, a][0], two[h][3])
            arrive(place(h, a, 2, None, 1), g_last[h, a][1], two[h][1])
        score(h, 2)

    offset = dp * 960
    lane = lax.broadcasted_iota(jnp.int32, (256, 128), 1)
    for h in range(2):
        mean = jnp.sum(squares[h], axis=1, keepdims=True) / D
        scaled = logits[h] / jnp.sqrt(mean + EPS)
        column = lax.broadcasted_iota(jnp.int32, (256, 960), 1) + offset
        stats = jnp.where(lane == 0, jnp.sum(jnp.exp(scaled), axis=1, keepdims=True), 0.0)
        for s in range(3):
            wanted = ids[h * 256 : (h + 1) * 256, s : s + 1]
            picked = jnp.sum(jnp.where(column == wanted, scaled, 0.0), axis=1, keepdims=True)
            stats = jnp.where(lane == s + 1, picked, stats)
        stat_a[0, :, h * 256 : (h + 1) * 256] = stats.T[:8]
    a_n = [None] + [send(stat_a.at[0], stat_a.at[d], z_peer[d]) for d in (1, 2, 3)]
    total = stat_a[0]
    for d in (1, 2, 3):
        arrive(stat_a.at[d], a_n[d], z_peer[4 - d])
        total = total + stat_a[d]
    stat_b[0, 0] = total
    b_n = {}
    for s in range(2):
        for d in range(4):
            if s or d:
                peer = far_peer[d] if s else y_peer[d]
                b_n[s, d] = send(stat_b.at[0, 0], stat_b.at[s, d], peer)
    for s in range(2):
        for d in range(4):
            if s or d:
                peer = far_peer[(4 - d) % 4] if s else y_peer[4 - d]
                arrive(stat_b.at[s, d], b_n[s, d], peer)
                total = total + stat_b[s, d]
    losses[...] = jnp.log(total[0:1]) - total[1:4]
    for copy in sent:
        copy.wait_send()


def shards(residual, partials, join_weight, head_weight, target_ids):
    vmem = pl.BlockSpec(memory_space=pltpu.VMEM)
    hbm = pl.BlockSpec(memory_space=pl.ANY)
    return pl.pallas_call(
        kernel,
        out_shape=jax.ShapeDtypeStruct((3, 512), F32),
        in_specs=[hbm, hbm, hbm, hbm, vmem],
        out_specs=vmem,
        scratch_shapes=[
            pltpu.VMEM((3, 64, 8192), BF16),
            pltpu.VMEM((3, 64, 2048), BF16),
            pltpu.VMEM((3, 2, 64, 2048), BF16),
            pltpu.VMEM((3, 64, 2048), BF16),
            pltpu.VMEM((3, 64, 2048), BF16),
            pltpu.VMEM((3, 4, 64, 512), BF16),
            pltpu.VMEM((3, 4, 2, 4, 64, 512), BF16),
            pltpu.VMEM((3, 4, 512, 256), BF16),
            pltpu.VMEM((960, 8192), BF16),
            pltpu.VMEM((2, 4, 2, 4, 64, 256), F32),
            pltpu.VMEM((4, 4, 2, 2, 64, 256), BF16),
            pltpu.VMEM((4, 4, 2, 2, 64, 256), BF16),
            pltpu.VMEM((4, 4, 2, 64, 256), BF16),
            pltpu.VMEM((4, 4, 2, 64, 256), BF16),
            pltpu.VMEM((4, 4, 2, 64, 256), BF16),
            pltpu.VMEM((4, 3, 2, 64, 256), BF16),
            pltpu.VMEM((4, 2, 64, 256), F32),
            pltpu.VMEM((4, 2, 4, 2, 4, 64, 256), BF16),
            pltpu.VMEM((2, 256, 960), F32),
            pltpu.VMEM((2, 256, 128), F32),
            pltpu.VMEM((4, 8, 512), F32),
            pltpu.VMEM((2, 4, 8, 512), F32),
            pltpu.SemaphoreType.DMA((COPIES,)),
            pltpu.SemaphoreType.DMA((COPIES,)),
            pltpu.SemaphoreType.DMA((8,)),
        ],
        compiler_params=pltpu.CompilerParams(
            collective_id=0, has_side_effects=True, vmem_limit_bytes=63 * 1024 * 1024
        ),
    )(residual, partials.reshape(3, 64, 8192), join_weight, head_weight.T, target_ids.T)


def solution(mesh):
    placed = (
        P(None, "dp", "tensor"),
        P(None, "dp", "tensor", None),
        P(None, "tensor", "dp"),
        P(None, "dp"),
        P(None, "tensor"),
    )
    return jax.shard_map(
        shards, mesh=mesh, in_specs=placed, out_specs=P(None, "tensor"), check_vma=False
    )
```

time: 779 us -> 192 us (0.25)
  waiting for transfers between devices: 386 us -> 0 us
  blocking collectives: 277 us -> 0 us
  Pallas kernels: 0 us -> 189 us
  local copies, waits for them, and re-layouts: 67.2 us -> 2.84 us
  matrix products: 27.9 us -> 0 us
  between operations: 13.2 us -> 0.01 us
    all_gather x2 -> x0, waiting for transfers between devices: 304 us -> none  [the longest x1 211 us: shards(): lax.all_gather(tap_values, 'dp', axis=1, tiled=True)]
    psum x2 -> x0, blocking collectives: 277 us -> none  [the longest x1 181 us: shards(): exp_sum, picked_sum = lax.psum((exp_total, picked), 'dp')]
    pallas_call x0 -> x1, Pallas kernels: none -> 189 us  [shards(): pl.pallas_call(kernel, out_shape=jax.ShapeDtypeStruct((3, 512), F32), in_...]
    gather x5 -> x0, local copies, waits for them, and re-layouts: 67.2 us -> none  [shards(): picked_raw = jnp.take_along_axis(logits, clipped.T, axis=1).T]
    reduce_scatter x1 -> x0, waiting for transfers between devices: 41.7 us -> none  [shards(): lax.psum_scatter(own_partial, 'tensor', scatter_dimension=2, tiled=True)]
    psum x1 -> x0, waiting for transfers between devices: 39.5 us -> none  [shards(): lax.psum(joined_part.astype(jnp.bfloat16), 'tensor').astype(jnp.float32)]
    dot_general x2 -> x0, matrix products: 27.9 us -> none  [the longest x1 15.1 us: shards(): jnp.dot(lax.all_gather(normed, 'dp', axis=1, tiled=True), head_weight, pr...]
  transfers between devices with their start and end apart: 4 -> 0, of which waited for: 4 -> 0; matrix products, arithmetic and copies ran while one was open for 0% -> 0% of each run, Pallas kernels for 0% -> 0%
where the time goes in v1:
time: 192 us
  Pallas kernels  189 us (98%)
  local copies, waits for them, and re-layouts  2.84 us (1%)
    pallas_call x1, Pallas kernels, shards(): pl.pallas_call(kernel, out_shape=jax.ShapeDtypeStruct((3, 512), F32), in_...  189 us

profile of v1, /device:TPU:0, one launch (start us, length us, event | category | flops | bytes accessed | tf_op | source)
XLA Modules:
  0.0 191.7 jit_solution(12564857282979380837)
XLA Ops:
  0.0 1.5 copy.6
  1.5 188.8 %shard_map.55 = f32[3,512]{1,0:T(4,128)} custom-call(bf16[3,64,2048]{2,1,0:T(8,128)(2,1)} %residual.1, bf16[3,64,8192]{2,1,0:T(8,128)(2,1)} %bitcast.4, bf16[3,2048,256]{2,1,0:T(8,128)(2,1)} %weight.1, bf16[960,8192]{1,0:T(8,128)(2,1)} %bitcast.3, s32[512,3]{1,0:T(8,128)} %bitcast.5), custom_call_target="tpu_custom_call" | custom-call | tf_op jit(solution)/shard_map/pallas_call | solution.py:383
  190.4 1.3 copy.8

commit v2 on v1

v2 whole, which is shorter than its diff:
```python
import jax
import jax.numpy as jnp
from jax import lax
from jax.experimental import pallas as pl
from jax.experimental.pallas import tpu as pltpu
from jax.sharding import PartitionSpec as P

D = 8192
EPS = 1e-05
F32 = jnp.float32
BF16 = jnp.bfloat16
COPIES = 280


def kernel(
    residual,
    partial,
    weight,
    head,
    ids,
    losses,
    part_v,
    res_v,
    sib_in,
    pair_out,
    pair_in,
    tap_out,
    taps,
    wz,
    head_v,
    acc,
    c_out,
    c_in,
    r_out,
    r_in,
    r_own,
    joined,
    logits,
    squares,
    stat_a,
    stat_b,
    send_sem,
    recv_sem,
    local_sem,
):
    dp = lax.axis_index("dp")
    t = lax.axis_index("tensor")
    z, xh, y = dp // 8, lax.rem(dp // 4, 2), lax.rem(dp, 4)
    xl, c = t // 2, lax.rem(t, 2)

    def device(zz, hh, yy, ll, cc):
        return (zz * 8 + hh * 4 + yy, ll * 2 + cc)

    def zo(d):
        return lax.rem(z + d, 4)

    def yo(d):
        return lax.rem(y + d, 4)

    sibling = device(z, xh, y, xl, 1 - c)
    pair = device(z, xh, y, 1 - xl, c)
    across = device(z, 1 - xh, y, xl, c)
    y_peer = [None] + [device(z, xh, yo(d), xl, c) for d in (1, 2, 3)]
    z_peer = [None] + [device(zo(d), xh, y, xl, c) for d in (1, 2, 3)]
    far_peer = [across] + [device(z, 1 - xh, yo(d), xl, c) for d in (1, 2, 3)]

    barrier = pltpu.get_barrier_semaphore()
    pair_z_peer = [pair] + [device(zo(d), xh, y, 1 - xl, c) for d in (1, 2, 3)]
    peers = [sibling] + y_peer[1:] + z_peer[1:] + far_peer + pair_z_peer
    for peer in peers:
        pl.semaphore_signal(barrier, inc=1, device_id=peer, device_id_type=pl.DeviceIdType.MESH)

    local = []

    def fetch(src, dst):
        copy = pltpu.make_async_copy(src, dst, local_sem.at[len(local)])
        copy.start()
        local.append(copy)
        return copy

    part_copy = [fetch(partial.at[k], part_v.at[k]) for k in range(3)]
    res_copy = fetch(residual, res_v)
    wz_copy = fetch(weight.at[:, pl.ds(pl.multiple_of(z * 512, 512), 512), :], wz.at[:, z])
    pl.semaphore_wait(barrier, len(peers))

    sent = []

    def make(src, dst, number, peer):
        return pltpu.make_async_remote_copy(
            src_ref=src,
            dst_ref=dst,
            send_sem=send_sem.at[number],
            recv_sem=recv_sem.at[number],
            device_id=peer,
            device_id_type=pl.DeviceIdType.MESH,
        )

    counter = iter(range(COPIES))

    def send(src, dst, peer, number=None):
        number = next(counter) if number is None else number
        copy = make(src, dst, number, peer)
        copy.start()
        sent.append(copy)
        return number

    def arrive(dst, number, peer):
        make(dst, dst, number, peer).wait_recv()

    sib_n = []
    for k in range(3):
        row = []
        for l in range(2):
            cols = pl.ds(pl.multiple_of((l * 2 + 1 - c) * 2048, 2048), 2048)
            row.append(send(partial.at[k, :, cols], sib_in.at[k, l], sibling))
        sib_n.append(row)
    wz_n = {}

    def swap(first, count):
        for d in (1, 2, 3):
            rows = pl.ds(pl.multiple_of(zo(d) * 512, 512), 512)
            taps_of = pl.ds(first, count)
            wz_n[first, d] = send(weight.at[taps_of, rows, :], wz.at[taps_of, z], z_peer[d])

    swap(0, 1)
    head_copy = fetch(head, head_v)

    own_cols = pl.ds(pl.multiple_of(t * 2048, 2048), 2048)
    pair_cols = pl.ds(pl.multiple_of(((1 - xl) * 2 + c) * 2048, 2048), 2048)
    pair_n = []
    for k in range(3):
        part_copy[k].wait()
        arrive(sib_in.at[k, 0], sib_n[k][0], sibling)
        arrive(sib_in.at[k, 1], sib_n[k][1], sibling)
        pair_out[k] = (part_v[k, :, pair_cols].astype(F32) + sib_in[k, 1 - xl].astype(F32)).astype(BF16)
        pair_n.append(send(pair_out.at[k], pair_in.at[k], pair))
    res_copy.wait()
    tap_n = {}
    far_n = {}
    ring_n = {}
    half_n = {}

    def make_taps(k):
        arrive(pair_in.at[k], pair_n[k], pair)
        tap = (
            res_v[k].astype(F32)
            + (part_v[k, :, own_cols].astype(F32) + sib_in[k, xl].astype(F32))
            + pair_in[k].astype(F32)
        ).astype(BF16)
        for q in range(4):
            tap_out[k, q] = tap[:, q * 512 : (q + 1) * 512]
        for d in (1, 2, 3):
            tap_n[k, d] = send(tap_out.at[k, zo(d)], taps.at[k, y, xh, z], z_peer[d])
        taps[k, y, xh, z] = tap_out[k, z]

    def gather(k):
        for d in (1, 2, 3):
            arrive(taps.at[k, y, xh, zo(4 - d)], tap_n[k, d], z_peer[4 - d])
        block = taps.at[k, y, xh]
        far_n[k] = send(block, block, across)
        ring_n[k, 0] = [send(block, block, y_peer[1]), send(block, block, y_peer[3])]

    def gather_far(k):
        arrive(taps.at[k, y, 1 - xh], far_n[k], across)
        block = taps.at[k, y, 1 - xh]
        ring_n[k, 1] = [send(block, block, y_peer[1]), send(block, block, y_peer[3])]

    def pass_on(k, h):
        hh = 1 - xh if h else xh
        arrive(taps.at[k, yo(3), hh], ring_n[k, h][0], y_peer[3])
        low = taps.at[k, yo(3), hh, pl.ds(0, 2)]
        first = send(low, low, y_peer[1])
        arrive(taps.at[k, yo(1), hh], ring_n[k, h][1], y_peer[1])
        high = taps.at[k, yo(1), hh, pl.ds(2, 2)]
        half_n[k, h] = [first, send(high, high, y_peer[3])]

    make_taps(0)
    make_taps(1)
    gather(0)
    make_taps(2)
    swap(1, 2)
    gather(1)
    gather_far(0)
    pass_on(0, 0)
    gather(2)
    for k in (1, 2):
        gather_far(k)
        pass_on(k, 0)

    chunk_y = [y, yo(3), yo(1), yo(2)]
    c_n, r_n = {}, {}

    def multiply(j):
        slot = j % 2
        row = chunk_y[j]

        @pl.loop(0, 4)
        def _(q):
            total = jnp.zeros((512, 256), F32)
            for k in range(3):
                total += jnp.dot(taps[k, row].reshape(512, 512), wz[k, q], preferred_element_type=F32)
            acc[slot, q] = total.reshape(2, 4, 64, 256)
            for l in range(2):
                c_out[j, q, :, l] = acc[slot, q, :, l * 2 + 1 - c].astype(BF16)

        c_n[j] = send(c_out.at[j], c_in.at[j], sibling)

    ways = [(l, d) for l in range(2) for d in range(4) if l or d]

    def over_core(j):
        slot = j % 2
        arrive(c_in.at[j], c_n[j], sibling)

        @pl.loop(0, 4)
        def _(q):
            for l in range(2):
                value = acc[slot, q, :, l * 2 + c] + c_in[j, q, :, l].astype(F32)
                r_out[j, l, q] = value.astype(BF16)

        for i, (l, d) in enumerate(ways):
            peer = pair_z_peer[d] if l else z_peer[d]
            ll = 1 - xl if l else xl
            r_n[j, i] = send(r_out.at[j, ll, zo(d)], r_in.at[j, i], peer)
        r_own[j] = acc[slot, z, :, t] + c_in[j, z, :, xl].astype(F32)

    def reduce(j):
        total = r_own[j]
        for i, (l, d) in enumerate(ways):
            arrive(r_in.at[j, i], r_n[j, i], pair_z_peer[(4 - d) % 4] if l else z_peer[4 - d])
            total = total + r_in[j, i].astype(F32)
        joined[z, xh, y, j] = total.astype(BF16)

    def last_taps():
        for h in range(2):
            hh = xh if h == 0 else 1 - xh
            for k in range(3):
                arrive(taps.at[k, yo(2), hh, pl.ds(0, 2)], half_n[k, h][0], y_peer[3])
                arrive(taps.at[k, yo(2), hh, pl.ds(2, 2)], half_n[k, h][1], y_peer[1])

    group = [pl.ds(0, 1), pl.ds(1, 2), pl.ds(3, 1)]
    one = [y_peer, z_peer]
    two = [z_peer, y_peer]
    g_far, g_ring, g_half, g_two, g_last = {}, {}, {}, {}, {}

    def place(g, h, a, b, ss=None, part=None):
        zz, yy = (zo(b), yo(a)) if h == 0 else (zo(a), yo(b))
        sl = slice(None) if ss is None else ss
        rows = slice(None) if part is None else pl.ds(part * 32, 32)
        return joined.at[zz, sl, yy, group[g], h, rows]

    def start_one(g, s):
        ss = xh if s == 0 else 1 - xh
        for h in range(2):
            block = place(g, h, 0, 0, ss)
            g_ring[g, h, s] = [send(block, block, one[h][1]), send(block, block, one[h][3])]

    def start_two(g, h, a):
        block = place(g, h, a, 0)
        g_two[g, h, a] = [send(block, block, two[h][1]), send(block, block, two[h][3])]

    def p_start(g):
        mine = joined.at[z, xh, y, group[g]]
        g_far[g] = send(mine, mine, across)
        start_one(g, 0)

    def p_far(g):
        arrive(joined.at[z, 1 - xh, y, group[g]], g_far[g], across)
        start_one(g, 1)
        for h in range(2):
            start_two(g, h, 0)

    def p_one(g):
        for s in range(2):
            ss = xh if s == 0 else 1 - xh
            for h in range(2):
                arrive(place(g, h, 3, 0, ss), g_ring[g, h, s][0], one[h][3])
                low = place(g, h, 3, 0, ss, 0)
                first = send(low, low, one[h][1])
                arrive(place(g, h, 1, 0, ss), g_ring[g, h, s][1], one[h][1])
                high = place(g, h, 1, 0, ss, 1)
                g_half[g, h, s] = [first, send(high, high, one[h][3])]
        for h in range(2):
            start_two(g, h, 3)
            start_two(g, h, 1)

    def p_one_far(g):
        for h in range(2):
            for s in range(2):
                ss = xh if s == 0 else 1 - xh
                arrive(place(g, h, 2, 0, ss, 0), g_half[g, h, s][0], one[h][3])
                arrive(place(g, h, 2, 0, ss, 1), g_half[g, h, s][1], one[h][1])
            start_two(g, h, 2)

    def p_two(g, a):
        for h in range(2):
            arrive(place(g, h, a, 3), g_two[g, h, a][0], two[h][3])
            low = place(g, h, a, 3, None, 0)
            first = send(low, low, two[h][1])
            arrive(place(g, h, a, 1), g_two[g, h, a][1], two[h][1])
            high = place(g, h, a, 1, None, 1)
            g_last[g, h, a] = [first, send(high, high, two[h][3])]

    def p_end(g):
        for h in range(2):
            for a in (0, 3, 1, 2):
                arrive(place(g, h, a, 2, None, 0), g_last[g, h, a][0], two[h][3])
                arrive(place(g, h, a, 2, None, 1), g_last[g, h, a][1], two[h][1])

    offsets = (0, 3, 1, 2)
    chunks = [(0,), (1, 2), (3,)]

    def score(g, first, count):
        n = len(chunks[g])

        @pl.loop(first, first + count)
        def _(yy):
            product = jnp.zeros((960, n * 128), F32)
            square = jnp.zeros((n * 128, 128), F32)
            for i in range(8):
                block = joined[i // 2, i % 2, yy, group[g]].reshape(n * 128, 256)
                cols = pl.ds(pl.multiple_of((i * 4 + yy) * 256, 256), 256)
                product += lax.dot_general(
                    head_v[:, cols], block, (((1,), (1,)), ((), ())), preferred_element_type=F32
                )
                wide = block.astype(F32)
                left, right = wide[:, :128], wide[:, 128:]
                square += left * left + right * right
            for p, j in enumerate(chunks[g]):
                row = lax.rem(yy + offsets[j], 4)
                logits[row] += product[:, p * 128 : (p + 1) * 128]
                squares[row] += square[p * 128 : (p + 1) * 128]

    logits[...] = jnp.zeros_like(logits)
    squares[...] = jnp.zeros_like(squares)
    wz_copy.wait()
    for d in (1, 2, 3):
        for first, count in ((0, 1), (1, 2)):
            arrive(wz.at[pl.ds(first, count), zo(4 - d)], wz_n[first, d], z_peer[4 - d])
    multiply(0)
    over_core(0)
    for k in range(3):
        pass_on(k, 1)
    multiply(1)
    over_core(1)
    reduce(0)
    p_start(0)
    multiply(2)
    p_far(0)
    over_core(2)
    p_one(0)
    reduce(1)
    reduce(2)
    p_start(1)
    last_taps()
    multiply(3)
    p_far(1)
    p_one_far(0)
    p_two(0, 0)
    over_core(3)
    p_one(1)
    p_two(0, 3)
    p_two(0, 1)
    p_two(0, 2)
    reduce(3)
    p_start(2)
    p_one_far(1)
    p_two(1, 0)
    p_far(2)
    p_two(1, 3)
    p_one(2)
    p_two(1, 1)
    head_copy.wait()
    p_end(0)
    score(0, 0, 2)
    p_one_far(2)
    p_two(2, 0)
    p_two(1, 2)
    score(0, 2, 2)
    p_two(2, 3)
    p_two(2, 1)
    p_two(2, 2)
    p_end(1)
    score(1, 0, 4)
    p_end(2)
    score(2, 0, 4)

    offset = dp * 960
    column = lax.broadcasted_iota(jnp.int32, (960, 128), 0) + offset
    blank = jnp.zeros((4, 128), F32)
    for row in range(4):
        mean = jnp.sum(squares[row].T, axis=0, keepdims=True) / D
        scaled = logits[row] / jnp.sqrt(mean + EPS)
        stats = [jnp.sum(jnp.exp(scaled), axis=0, keepdims=True)]
        for s in range(3):
            wanted = ids[row, s : s + 1]
            stats.append(jnp.sum(jnp.where(column == wanted, scaled, 0.0), axis=0, keepdims=True))
        stat_a[0, :, row * 128 : (row + 1) * 128] = jnp.concatenate(stats + [blank], axis=0)
    a_n = [None] + [send(stat_a.at[0], stat_a.at[d], z_peer[d]) for d in (1, 2, 3)]
    total = stat_a[0]
    for d in (1, 2, 3):
        arrive(stat_a.at[d], a_n[d], z_peer[4 - d])
        total = total + stat_a[d]
    stat_b[0, 0] = total
    b_n = {}
    for s in range(2):
        for d in range(4):
            if s or d:
                peer = far_peer[d] if s else y_peer[d]
                b_n[s, d] = send(stat_b.at[0, 0], stat_b.at[s, d], peer)
    for s in range(2):
        for d in range(4):
            if s or d:
                peer = far_peer[(4 - d) % 4] if s else y_peer[4 - d]
                arrive(stat_b.at[s, d], b_n[s, d], peer)
                total = total + stat_b[s, d]
    losses[...] = jnp.log(total[0:1]) - total[1:4]
    for copy in sent:
        copy.wait_send()


def shards(residual, partials, join_weight, head_weight, target_ids):
    vmem = pl.BlockSpec(memory_space=pltpu.VMEM)
    hbm = pl.BlockSpec(memory_space=pl.ANY)
    ids = target_ids.reshape(3, 2, 4, 64).transpose(2, 0, 1, 3).reshape(4, 3, 128)
    result = pl.pallas_call(
        kernel,
        out_shape=jax.ShapeDtypeStruct((3, 512), F32),
        in_specs=[hbm, hbm, hbm, hbm, vmem],
        out_specs=vmem,
        scratch_shapes=[
            pltpu.VMEM((3, 64, 8192), BF16),
            pltpu.VMEM((3, 64, 2048), BF16),
            pltpu.VMEM((3, 2, 64, 2048), BF16),
            pltpu.VMEM((3, 64, 2048), BF16),
            pltpu.VMEM((3, 64, 2048), BF16),
            pltpu.VMEM((3, 4, 64, 512), BF16),
            pltpu.VMEM((3, 4, 2, 4, 64, 512), BF16),
            pltpu.VMEM((3, 4, 512, 256), BF16),
            pltpu.VMEM((960, 8192), BF16),
            pltpu.VMEM((2, 4, 2, 4, 64, 256), F32),
            pltpu.VMEM((4, 4, 2, 2, 64, 256), BF16),
            pltpu.VMEM((4, 4, 2, 2, 64, 256), BF16),
            pltpu.VMEM((4, 2, 4, 2, 64, 256), BF16),
            pltpu.VMEM((4, 7, 2, 64, 256), BF16),
            pltpu.VMEM((4, 2, 64, 256), F32),
            pltpu.VMEM((4, 2, 4, 4, 2, 64, 256), BF16),
            pltpu.VMEM((4, 960, 128), F32),
            pltpu.VMEM((4, 128, 128), F32),
            pltpu.VMEM((4, 8, 512), F32),
            pltpu.VMEM((2, 4, 8, 512), F32),
            pltpu.SemaphoreType.DMA((COPIES,)),
            pltpu.SemaphoreType.DMA((COPIES,)),
            pltpu.SemaphoreType.DMA((8,)),
        ],
        compiler_params=pltpu.CompilerParams(
            collective_id=0, has_side_effects=True, vmem_limit_bytes=63 * 1024 * 1024
        ),
    )(residual, partials.reshape(3, 64, 8192), join_weight, head_weight.T, ids)
    return result.reshape(3, 4, 2, 64).transpose(0, 2, 1, 3).reshape(3, 512)


def solution(mesh):
    placed = (
        P(None, "dp", "tensor"),
        P(None, "dp", "tensor", None),
        P(None, "tensor", "dp"),
        P(None, "dp"),
        P(None, "tensor"),
    )
    return jax.shard_map(
        shards, mesh=mesh, in_specs=placed, out_specs=P(None, "tensor"), check_vma=False
    )
```

time: 192 us -> 165 us (0.86)
  Pallas kernels: 189 us -> 161 us
    pallas_call x1, Pallas kernels: 189 us -> 161 us  [shards(): pl.pallas_call(kernel, out_shape=jax.ShapeDtypeStruct((3, 512), F32), in_...]
    reshape x0 -> x6, local copies, waits for them, and re-layouts: none -> 2.95 us  [the longest x4 1.48 us: shards(): target_ids.reshape(3, 2, 4, 64).transpose(2, 0, 1, 3).reshape(4, 3, 128)]
    unnamed x2 -> x0, local copies, waits for them, and re-layouts: 2.84 us -> none
where the time goes in v2:
time: 165 us; the launch traced here: 164 us
  Pallas kernels  161 us (98%)
  local copies, waits for them, and re-layouts  2.96 us (2%)
    pallas_call x1, Pallas kernels, shards(): pl.pallas_call(kernel, out_shape=jax.ShapeDtypeStruct((3, 512), F32), in_...  161 us

profile of v2, /device:TPU:0, one launch (start us, length us, event | category | flops | bytes accessed | tf_op | source)
XLA Modules:
  0.0 164.3 jit_solution(10537288593431940755)
XLA Ops:
  0.0 0.8 reshape.16
  0.8 0.1 reshape.17
  0.9 0.6 copy.9.ids
  1.5 161.3 %shard_map.55 = f32[3,512]{1,0:T(4,128)} custom-call(bf16[3,64,2048]{2,1,0:T(8,128)(2,1)} %residual.1, bf16[3,64,8192]{2,1,0:T(8,128)(2,1)} %bitcast.9, bf16[3,2048,256]{2,1,0:T(8,128)(2,1)} %weight.1, bf16[960,8192]{1,0:T(8,128)(2,1)} %bitcast.8, s32[4,3,128]{2,1,0:T(4,128)} %copy.9.ids), custom_call_target="tpu_custom_call" | custom-call | tf_op jit(solution)/shard_map/pallas_call | solution.py:425
  162.8 0.8 reshape.18
  163.6 0.7 reshape.19
  (2 shorter events, 0.0 us)

commit v3 on v2

--- a/solution.py
+++ b/solution.py
@@ -9,7 +9,7 @@
 EPS = 1e-05
 F32 = jnp.float32
 BF16 = jnp.bfloat16
-COPIES = 280
+COPIES = 360
 
 
 def kernel(
@@ -116,13 +116,16 @@
         sib_n.append(row)
     wz_n = {}
 
-    def swap(first, count):
+    swaps = [(0, 0, 4), (1, 0, 1), (1, 1, 1), (1, 2, 2), (2, 0, 4)]
+
+    def swap(n):
+        k, first, count = swaps[n]
         for d in (1, 2, 3):
-            rows = pl.ds(pl.multiple_of(zo(d) * 512, 512), 512)
-            taps_of = pl.ds(first, count)
-            wz_n[first, d] = send(weight.at[taps_of, rows, :], wz.at[taps_of, z], z_peer[d])
-
-    swap(0, 1)
+            rows = pl.ds(pl.multiple_of(zo(d) * 512 + first * 128, 128), count * 128)
+            landing = pl.ds(first * 128, count * 128)
+            wz_n[n, d] = send(weight.at[k, rows, :], wz.at[k, z, landing], z_peer[d])
+
+    swap(0)
     head_copy = fetch(head, head_v)
 
     own_cols = pl.ds(pl.multiple_of(t * 2048, 2048), 2048)
@@ -175,17 +178,18 @@
         half_n[k, h] = [first, send(high, high, y_peer[3])]
 
     make_taps(0)
+    swap(1)
     make_taps(1)
+    swap(2)
     gather(0)
     make_taps(2)
-    swap(1, 2)
+    swap(3)
+    swap(4)
     gather(1)
     gather_far(0)
-    pass_on(0, 0)
     gather(2)
-    for k in (1, 2):
-        gather_far(k)
-        pass_on(k, 0)
+    gather_far(1)
+    gather_far(2)
 
     chunk_y = [y, yo(3), yo(1), yo(2)]
     c_n, r_n = {}, {}
@@ -237,7 +241,8 @@
                 arrive(taps.at[k, yo(2), hh, pl.ds(0, 2)], half_n[k, h][0], y_peer[3])
                 arrive(taps.at[k, yo(2), hh, pl.ds(2, 2)], half_n[k, h][1], y_peer[1])
 
-    group = [pl.ds(0, 1), pl.ds(1, 2), pl.ds(3, 1)]
+    group = [pl.ds(j, 1) for j in range(4)]
+    spans = [pl.ds(0, 1), pl.ds(1, 2), pl.ds(3, 1)]
     one = [y_peer, z_peer]
     two = [z_peer, y_peer]
     g_far, g_ring, g_half, g_two, g_last = {}, {}, {}, {}, {}
@@ -317,7 +322,7 @@
             product = jnp.zeros((960, n * 128), F32)
             square = jnp.zeros((n * 128, 128), F32)
             for i in range(8):
-                block = joined[i // 2, i % 2, yy, group[g]].reshape(n * 128, 256)
+                block = joined[i // 2, i % 2, yy, spans[g]].reshape(n * 128, 256)
                 cols = pl.ds(pl.multiple_of((i * 4 + yy) * 256, 256), 256)
                 product += lax.dot_general(
                     head_v[:, cols], block, (((1,), (1,)), ((), ())), preferred_element_type=F32
@@ -334,12 +339,13 @@
     squares[...] = jnp.zeros_like(squares)
     wz_copy.wait()
     for d in (1, 2, 3):
-        for first, count in ((0, 1), (1, 2)):
-            arrive(wz.at[pl.ds(first, count), zo(4 - d)], wz_n[first, d], z_peer[4 - d])
+        for n, (k, first, count) in enumerate(swaps):
+            arrive(wz.at[k, zo(4 - d), pl.ds(first * 128, count * 128)], wz_n[n, d], z_peer[4 - d])
     multiply(0)
     over_core(0)
-    for k in range(3):
-        pass_on(k, 1)
+    for h in range(2):
+        for k in range(3):
+            pass_on(k, h)
     multiply(1)
     over_core(1)
     reduce(0)
@@ -349,52 +355,63 @@
     over_core(2)
     p_one(0)
     reduce(1)
+    p_start(1)
     reduce(2)
-    p_start(1)
-    last_taps()
-    multiply(3)
+    p_start(2)
     p_far(1)
     p_one_far(0)
     p_two(0, 0)
+    last_taps()
+    multiply(3)
+    p_far(2)
+    p_one(1)
     over_core(3)
-    p_one(1)
     p_two(0, 3)
     p_two(0, 1)
     p_two(0, 2)
-    reduce(3)
-    p_start(2)
+    p_one(2)
     p_one_far(1)
     p_two(1, 0)
-    p_far(2)
+    reduce(3)
+    p_start(3)
+    p_one_far(2)
+    p_two(2, 0)
     p_two(1, 3)
-    p_one(2)
     p_two(1, 1)
+    p_far(3)
+    p_two(2, 3)
+    p_two(2, 1)
+    p_one(3)
+    p_two(1, 2)
     head_copy.wait()
     p_end(0)
     score(0, 0, 2)
-    p_one_far(2)
-    p_two(2, 0)
-    p_two(1, 2)
+    p_two(2, 2)
+    p_one_far(3)
+    p_two(3, 0)
     score(0, 2, 2)
-    p_two(2, 3)
-    p_two(2, 1)
-    p_two(2, 2)
+    p_two(3, 3)
+    p_two(3, 1)
+    p_two(3, 2)
     p_end(1)
+    p_end(2)
     score(1, 0, 4)
-    p_end(2)
+    p_end(3)
     score(2, 0, 4)
 
     offset = dp * 960
     column = lax.broadcasted_iota(jnp.int32, (960, 128), 0) + offset
-    blank = jnp.zeros((4, 128), F32)
+    every = []
     for row in range(4):
         mean = jnp.sum(squares[row].T, axis=0, keepdims=True) / D
         scaled = logits[row] / jnp.sqrt(mean + EPS)
-        stats = [jnp.sum(jnp.exp(scaled), axis=0, keepdims=True)]
+        every.append(jnp.sum(jnp.exp(scaled), axis=0, keepdims=True))
         for s in range(3):
-            wanted = ids[row, s : s + 1]
-            stats.append(jnp.sum(jnp.where(column == wanted, scaled, 0.0), axis=0, keepdims=True))
-        stat_a[0, :, row * 128 : (row + 1) * 128] = jnp.concatenate(stats + [blank], axis=0)
+            low = ids[s : s + 1, row * 64 : row * 64 + 64]
+            high = ids[s : s + 1, 256 + row * 64 : 256 + row * 64 + 64]
+            wanted = jnp.concatenate([low, high], axis=1)
+            every.append(jnp.sum(jnp.where(column == wanted, scaled, 0.0), axis=0, keepdims=True))
+    stat_a[0] = jnp.concatenate(every, axis=0)
     a_n = [None] + [send(stat_a.at[0], stat_a.at[d], z_peer[d]) for d in (1, 2, 3)]
     total = stat_a[0]
     for d in (1, 2, 3):
@@ -413,7 +430,8 @@
                 peer = far_peer[(4 - d) % 4] if s else y_peer[4 - d]
                 arrive(stat_b.at[s, d], b_n[s, d], peer)
                 total = total + stat_b[s, d]
-    losses[...] = jnp.log(total[0:1]) - total[1:4]
+    loss = [jnp.log(total[row * 4 : row * 4 + 1]) - total[row * 4 + 1 : row * 4 + 4] for row in range(4)]
+    losses[...] = jnp.concatenate([v[:, :64] for v in loss] + [v[:, 64:] for v in loss], axis=1)
     for copy in sent:
         copy.wait_send()
 
@@ -421,8 +439,7 @@
 def shards(residual, partials, join_weight, head_weight, target_ids):
     vmem = pl.BlockSpec(memory_space=pltpu.VMEM)
     hbm = pl.BlockSpec(memory_space=pl.ANY)
-    ids = target_ids.reshape(3, 2, 4, 64).transpose(2, 0, 1, 3).reshape(4, 3, 128)
-    result = pl.pallas_call(
+    return pl.pallas_call(
         kernel,
         out_shape=jax.ShapeDtypeStruct((3, 512), F32),
         in_specs=[hbm, hbm, hbm, hbm, vmem],
@@ -446,8 +463,8 @@
             pltpu.VMEM((4, 2, 4, 4, 2, 64, 256), BF16),
             pltpu.VMEM((4, 960, 128), F32),
             pltpu.VMEM((4, 128, 128), F32),
-            pltpu.VMEM((4, 8, 512), F32),
-            pltpu.VMEM((2, 4, 8, 512), F32),
+            pltpu.VMEM((4, 16, 128), F32),
+            pltpu.VMEM((2, 4, 16, 128), F32),
             pltpu.SemaphoreType.DMA((COPIES,)),
             pltpu.SemaphoreType.DMA((COPIES,)),
             pltpu.SemaphoreType.DMA((8,)),
@@ -455,8 +472,7 @@
         compiler_params=pltpu.CompilerParams(
             collective_id=0, has_side_effects=True, vmem_limit_bytes=63 * 1024 * 1024
         ),
-    )(residual, partials.reshape(3, 64, 8192), join_weight, head_weight.T, ids)
-    return result.reshape(3, 4, 2, 64).transpose(0, 2, 1, 3).reshape(3, 512)
+    )(residual, partials.reshape(3, 64, 8192), join_weight, head_weight.T, target_ids)
 
 
 def solution(mesh):

time: 165 us -> 156 us (0.945)
  Pallas kernels: 161 us -> 154 us
  local copies, waits for them, and re-layouts: 2.96 us -> 1.3 us
    pallas_call x1, Pallas kernels: 161 us -> 154 us  [shards(): pl.pallas_call(kernel, out_shape=jax.ShapeDtypeStruct((3, 512), F32), in_...]
    reshape x6 -> x0, local copies, waits for them, and re-layouts: 2.95 us -> none  [the longest x4 1.48 us: shards(): target_ids.reshape(3, 2, 4, 64).transpose(2, 0, 1, 3).reshape(4, 3, 128)]
where the time goes in v3:
time: 156 us
  Pallas kernels  154 us (99%)
    pallas_call x1, Pallas kernels, shards(): pl.pallas_call(kernel, out_shape=jax.ShapeDtypeStruct((3, 512), F32), in_...  154 us

profile of v3, /device:TPU:0, one launch (start us, length us, event | category | flops | bytes accessed | tf_op | source)
XLA Modules:
  0.0 155.7 jit_solution(17120928024661613844)
XLA Ops:
  0.0 154.4 %shard_map.55 = f32[3,512]{1,0:T(4,128)} custom-call(bf16[3,64,2048]{2,1,0:T(8,128)(2,1)} %residual.1, bf16[3,64,8192]{2,1,0:T(8,128)(2,1)} %bitcast.3, bf16[3,2048,256]{2,1,0:T(8,128)(2,1)} %weight.1, bf16[960,8192]{1,0:T(8,128)(2,1)} %bitcast.2, s32[3,512]{1,0:T(4,128)} %ids.1), custom_call_target="tpu_custom_call" | custom-call | tf_op jit(solution)/shard_map/pallas_call | solution.py:442
  154.4 1.3 copy.7

commit v4 on v3

--- a/solution.py
+++ b/solution.py
@@ -130,66 +130,80 @@
 
     own_cols = pl.ds(pl.multiple_of(t * 2048, 2048), 2048)
     pair_cols = pl.ds(pl.multiple_of(((1 - xl) * 2 + c) * 2048, 2048), 2048)
-    pair_n = []
-    for k in range(3):
-        part_copy[k].wait()
-        arrive(sib_in.at[k, 0], sib_n[k][0], sibling)
-        arrive(sib_in.at[k, 1], sib_n[k][1], sibling)
-        pair_out[k] = (part_v[k, :, pair_cols].astype(F32) + sib_in[k, 1 - xl].astype(F32)).astype(BF16)
-        pair_n.append(send(pair_out.at[k], pair_in.at[k], pair))
-    res_copy.wait()
-    tap_n = {}
-    far_n = {}
-    ring_n = {}
-    half_n = {}
-
-    def make_taps(k):
-        arrive(pair_in.at[k], pair_n[k], pair)
+    pieces = [(0, 0, 32), (0, 32, 32), (1, 0, 64), (2, 0, 64)]
+    pair_n, tap_n, far_n, ring_n, half_n = {}, {}, {}, {}, {}
+
+    def block_of(p, yy, hh, zz=slice(None)):
+        k, first, count = pieces[p]
+        return taps.at[k, yy, hh, zz, pl.ds(first, count)]
+
+    def send_pair(p):
+        k, first, count = pieces[p]
+        rows = pl.ds(first, count)
+        if first == 0:
+            part_copy[k].wait()
+            arrive(sib_in.at[k, 0], sib_n[k][0], sibling)
+            arrive(sib_in.at[k, 1], sib_n[k][1], sibling)
+        pair_out[k, rows] = (
+            part_v[k, rows, pair_cols].astype(F32) + sib_in[k, 1 - xl, rows].astype(F32)
+        ).astype(BF16)
+        pair_n[p] = send(pair_out.at[k, rows], pair_in.at[k, rows], pair)
+
+    def make_taps(p):
+        k, first, count = pieces[p]
+        rows = pl.ds(first, count)
+        arrive(pair_in.at[k, rows], pair_n[p], pair)
         tap = (
-            res_v[k].astype(F32)
-            + (part_v[k, :, own_cols].astype(F32) + sib_in[k, xl].astype(F32))
-            + pair_in[k].astype(F32)
+            res_v[k, rows].astype(F32)
+            + (part_v[k, rows, own_cols].astype(F32) + sib_in[k, xl, rows].astype(F32))
+            + pair_in[k, rows].astype(F32)
         ).astype(BF16)
         for q in range(4):
-            tap_out[k, q] = tap[:, q * 512 : (q + 1) * 512]
+            tap_out[k, q, rows] = tap[:, q * 512 : (q + 1) * 512]
         for d in (1, 2, 3):
-            tap_n[k, d] = send(tap_out.at[k, zo(d)], taps.at[k, y, xh, z], z_peer[d])
-        taps[k, y, xh, z] = tap_out[k, z]
-
-    def gather(k):
+            tap_n[p, d] = send(tap_out.at[k, zo(d), rows], block_of(p, y, xh, z), z_peer[d])
+        taps[k, y, xh, z, rows] = tap_out[k, z, rows]
+
+    def gather(p):
         for d in (1, 2, 3):
-            arrive(taps.at[k, y, xh, zo(4 - d)], tap_n[k, d], z_peer[4 - d])
-        block = taps.at[k, y, xh]
-        far_n[k] = send(block, block, across)
-        ring_n[k, 0] = [send(block, block, y_peer[1]), send(block, block, y_peer[3])]
-
-    def gather_far(k):
-        arrive(taps.at[k, y, 1 - xh], far_n[k], across)
-        block = taps.at[k, y, 1 - xh]
-        ring_n[k, 1] = [send(block, block, y_peer[1]), send(block, block, y_peer[3])]
-
-    def pass_on(k, h):
+            arrive(block_of(p, y, xh, zo(4 - d)), tap_n[p, d], z_peer[4 - d])
+        block = block_of(p, y, xh)
+        far_n[p] = send(block, block, across)
+        ring_n[p, 0] = [send(block, block, y_peer[1]), send(block, block, y_peer[3])]
+
+    def gather_far(p):
+        block = block_of(p, y, 1 - xh)
+        arrive(block, far_n[p], across)
+        ring_n[p, 1] = [send(block, block, y_peer[1]), send(block, block, y_peer[3])]
+
+    def pass_on(p, h):
         hh = 1 - xh if h else xh
-        arrive(taps.at[k, yo(3), hh], ring_n[k, h][0], y_peer[3])
-        low = taps.at[k, yo(3), hh, pl.ds(0, 2)]
+        arrive(block_of(p, yo(3), hh), ring_n[p, h][0], y_peer[3])
+        low = block_of(p, yo(3), hh, pl.ds(0, 2))
         first = send(low, low, y_peer[1])
-        arrive(taps.at[k, yo(1), hh], ring_n[k, h][1], y_peer[1])
-        high = taps.at[k, yo(1), hh, pl.ds(2, 2)]
-        half_n[k, h] = [first, send(high, high, y_peer[3])]
-
+        arrive(block_of(p, yo(1), hh), ring_n[p, h][1], y_peer[1])
+        high = block_of(p, yo(1), hh, pl.ds(2, 2))
+        half_n[p, h] = [first, send(high, high, y_peer[3])]
+
+    for p in range(4):
+        send_pair(p)
+    res_copy.wait()
     make_taps(0)
+    make_taps(1)
     swap(1)
-    make_taps(1)
-    swap(2)
     gather(0)
     make_taps(2)
+    swap(2)
+    gather(1)
+    make_taps(3)
+    gather(2)
     swap(3)
     swap(4)
-    gather(1)
     gather_far(0)
-    gather(2)
     gather_far(1)
+    gather(3)
     gather_far(2)
+    gather_far(3)
 
     chunk_y = [y, yo(3), yo(1), yo(2)]
     c_n, r_n = {}, {}
@@ -237,9 +251,9 @@
     def last_taps():
         for h in range(2):
             hh = xh if h == 0 else 1 - xh
-            for k in range(3):
-                arrive(taps.at[k, yo(2), hh, pl.ds(0, 2)], half_n[k, h][0], y_peer[3])
-                arrive(taps.at[k, yo(2), hh, pl.ds(2, 2)], half_n[k, h][1], y_peer[1])
+            for p in range(4):
+                arrive(block_of(p, yo(2), hh, pl.ds(0, 2)), half_n[p, h][0], y_peer[3])
+                arrive(block_of(p, yo(2), hh, pl.ds(2, 2)), half_n[p, h][1], y_peer[1])
 
     group = [pl.ds(j, 1) for j in range(4)]
     spans = [pl.ds(0, 1), pl.ds(1, 2), pl.ds(3, 1)]
@@ -344,23 +358,23 @@
     multiply(0)
     over_core(0)
     for h in range(2):
-        for k in range(3):
-            pass_on(k, h)
+        for p in range(4):
+            pass_on(p, h)
     multiply(1)
-    over_core(1)
     reduce(0)
     p_start(0)
+    over_core(1)
     multiply(2)
     p_far(0)
     over_core(2)
     p_one(0)
     reduce(1)
     p_start(1)
+    p_one_far(0)
+    p_two(0, 0)
     reduce(2)
     p_start(2)
     p_far(1)
-    p_one_far(0)
-    p_two(0, 0)
     last_taps()
     multiply(3)
     p_far(2)

time: 156 us -> 153 us (0.981)
  Pallas kernels: 154 us -> 151 us
    pallas_call x1, Pallas kernels: 154 us -> 151 us  [shards(): pl.pallas_call(kernel, out_shape=jax.ShapeDtypeStruct((3, 512), F32), in_...]
where the time goes in v4:
time: 153 us
  Pallas kernels  151 us (99%)
    pallas_call x1, Pallas kernels, shards(): pl.pallas_call(kernel, out_shape=jax.ShapeDtypeStruct((3, 512), F32), in_...  151 us

profile of v4, /device:TPU:0, one launch (start us, length us, event | category | flops | bytes accessed | tf_op | source)
XLA Modules:
  0.0 152.8 jit_solution(4589248555278514663)
XLA Ops:
  0.0 151.5 %shard_map.55 = f32[3,512]{1,0:T(4,128)} custom-call(bf16[3,64,2048]{2,1,0:T(8,128)(2,1)} %residual.1, bf16[3,64,8192]{2,1,0:T(8,128)(2,1)} %bitcast.3, bf16[3,2048,256]{2,1,0:T(8,128)(2,1)} %weight.1, bf16[960,8192]{1,0:T(8,128)(2,1)} %bitcast.2, s32[3,512]{1,0:T(4,128)} %ids.1), custom_call_target="tpu_custom_call" | custom-call | tf_op jit(solution)/shard_map/pallas_call | solution.py:456
  151.5 1.3 copy.7
